TPU v7x, 32 devices: a whole 2x2x4 slice. The times are simulated.
32 devices in a mesh: light: 4 (over y, core), view: 8 (over z, x).
Axes of the slice: x: 2, y: 2, z: 4, core: 2. Of those that a mesh axis runs over, the one named last changes fastest.
Arguments:
- density: float32 [128, 32, 4096], P('light', 'view'), may hold values from 0.1 to 8
- emission: float32 [128, 32, 4096], P('light', 'view'), may hold values from 0.1 to 1
- facing: int32 [128], P('light'), may hold values 0 or 1
Outputs:
- radiance: float32 [128, 4096], P('light', 'view')
- coverage: float32 [128, 4096], P('light', 'view')
All inputs are finite; a program needn't handle non-finite values. No bound on the sum of `facing` on one device may be relied on, other than what follows from the above.
Results may differ from a plain program's by a relative error of at most 0.0003.
Values sent between devices are 32-bit elements; how exact they have to be, the bound alone decides.
A program may use at most 64 MiB of HBM per device.

v0:
```python
import jax
import jax.numpy as jnp
from jax import lax
from jax.sharding import PartitionSpec as P


def entering(value, axis, join, neutral):
    count, mine = (lax.axis_size(axis), lax.axis_index(axis))
    pieces = lax.all_gather(value, axis)
    so_far = jnp.full_like(value, 0) + jnp.asarray(neutral, value.dtype)

    def hop(position, so_far):
        longer = join(so_far, pieces[position])
        return jnp.where(position < mine, longer, so_far)

    return lax.fori_loop(0, count - 1, hop, so_far)


def swapped(value, axis, bit):
    return lax.ppermute(value, axis, [(i, i ^ 1 << bit) for i in range(lax.axis_size(axis))])


def shards(density, emission, facing):
    rows, depth_cells, columns = density.shape
    light_count = lax.axis_size("light")
    view_count = lax.axis_size("view")
    tau_light = density * (1.0 / (rows * light_count))
    tau_view = density * (1.0 / (depth_cells * view_count))
    slab_depth = jnp.sum(tau_light, axis=0)
    incoming = entering(
        slab_depth, "light", lambda early, late: early + late, jnp.zeros_like(slab_depth)
    )
    depth = incoming[None] + (jnp.cumsum(tau_light, axis=0) - tau_light)
    lit = emission * (0.2 + jnp.exp(-depth)) * (1.0 - jnp.exp(-tau_view))
    running = jnp.cumsum(tau_view, axis=1)
    total = jnp.sum(tau_view, axis=1)
    forward = jnp.sum(lit * jnp.exp(-(running - tau_view)), axis=1)
    backward = jnp.sum(lit * jnp.exp(-(total[:, None, :] - running)), axis=1)
    reversed_rows = facing == 1
    color = jnp.where(reversed_rows[:, None], backward, forward)
    trans = jnp.exp(-total)
    block_width = columns // view_count
    stacked = jnp.stack([color, trans]).reshape(2, rows, view_count, block_width)
    my_view = lax.axis_index("view")
    for bit in range(view_count.bit_length() - 1):
        blocks = stacked.shape[2]
        paired = stacked.reshape(2, rows, blocks // 2, 2, block_width)
        my_bit = my_view >> bit & 1
        keep_part = jnp.where(my_bit == 1, paired[:, :, :, 1], paired[:, :, :, 0])
        send_part = jnp.where(my_bit == 1, paired[:, :, :, 0], paired[:, :, :, 1])
        partner = swapped(send_part, "view", bit)
        in_front = ((my_bit == 0) == jnp.logical_not(reversed_rows))[:, None, None]
        front_part = jnp.where(in_front, keep_part, partner)
        back_part = jnp.where(in_front, partner, keep_part)
        stacked = jnp.stack(
            [front_part[0] + front_part[1] * back_part[0], front_part[1] * back_part[1]]
        )
    radiance = stacked[0][:, 0]
    coverage = stacked[1][:, 0]
    return (radiance, coverage)


def solution(mesh):
    return jax.shard_map(
        shards,
        mesh=mesh,
        in_specs=(P("light", "view", None), P("light", "view", None), P("light")),
        out_specs=(P("light", "view"), P("light", "view")),
        check_vma=False,
    )
```

profile of v0, /device:TPU:0, one launch (start us, length us, event | category | flops | bytes accessed | tf_op | source)
XLA Modules:
  0.0 63.0 jit_solution(17818007136614401635)
XLA Ops:
  0.7 4.0 %multiply_reduce_fusion.2 = (f32[4,4096]{1,0:T(4,128)S(1)}, f32[32,4096]{1,0:T(8,128)S(1)}, f32[32,4,4096]{2,1,0:T(4,128)}) fusion(f32[32,4,4096]{2,1,0:T(4,128)} %param.5), kind=kLoop, calls=%fused_computation.6 | loop fusion | flops 1949696 | bytes 4784128 | tf_op jit(solution)/shard_map/reduce_sum | solution.py:29
  4.7 7.2 %all-gather.1 = f32[4,4,4096]{2,1,0:T(4,128)S(1)} all-gather(f32[1,4,4096]{2,1,0:T(4,128)S(1)} %bitcast.79), channel_id=2, replica_groups=mesh['light'=4,'view'=8] {'light'}, dimensions={0}, use_global_device_ids=true | all-gather | bytes 327680 | tf_op jit(solution)/shard_map/all_gather | solution.py:9
  11.9 0.2 while.14
  11.9 0.1 add_select_fusion.2
  12.0 0.1 add_select_fusion.2
  12.1 0.1 add_select_fusion.2
  12.1 0.9 %negate_exponential_fusion = f32[32,4096]{1,0:T(8,128)} fusion(f32[32,4096]{1,0:T(8,128)S(1)} %get-tuple-element.100), kind=kLoop, calls=%fused_computation.19 | loop fusion | flops 131072 | bytes 1048576 | tf_op jit(solution)/shard_map/exp | solution.py:41
  13.0 0.0 copy-start
  13.0 6.6 %reduce_window_sum.23 = f32[32,4,4096]{2,1,0:T(4,128)} reduce-window(f32[32,4,4096]{2,1,0:T(4,128)} %get-tuple-element.112, f32[]{:T(128)} %constant.48.clone.1), window={size=1x4x1 pad=0_0x3_0x0_0}, to_apply=%region_5.6 | reduce-window | flops 1572864 | bytes 4194308 | tf_op jit(solution)/shard_map/jit(cumsum)/reduce_window_sum | solution.py:35
  19.6 0.0 copy-done
  19.6 7.7 %multiply_reduce_fusion = (f32[32,4096]{1,0:T(8,128)S(1)}, f32[32,4096]{1,0:T(8,128)}) fusion(f32[32,4,4096]{2,1,0:T(4,128)} %reduce_window_sum.23, f32[32,4,4096]{2,1,0:T(4,128)S(1)} %copy-done, f32[32,4096]{1,0:T(8,128)S(1)} %get-tuple-element.100, f32[32,4,4096]{2,1,0:T(4,128)} %param.6, f32[4,4096]{1,0:T(4,128)S(1)} %get-tuple-element.81), kind=kOutput, calls=%fused_computation.1 | output fusion | flops 25952256 | bytes 7929856 | tf_op jit(solution)/shard_map/jit(cumsum)/reduce_window_sum | solution.py:33
  27.4 0.0 copy-start.1
  27.4 0.0 copy-start.2
  27.4 1.5 %reduce_sum.43 = f32[1,32,4,2,512]{4,3,2,1,0:T(2,128)S(1)} reshape(f32[32,4096]{1,0:T(8,128)} %get-tuple-element.98) | data formatting | bytes 1048576 | tf_op jit(solution)/shard_map/reduce_sum | solution.py:38
  28.9 0.4 reduce_sum.45
  29.4 0.0 copy-done.1
  29.4 0.4 exp.31
  29.8 0.0 copy-done.2
  29.8 0.3 broadcast_select_fusion.1
  30.2 1.1 %broadcast_select_fusion = (f32[2,32,4,1,512]{4,3,2,1,0:T(1,128)S(1)}, f32[2,32,4,1,512]{4,3,2,1,0:T(1,128)S(1)}, f32[2,32,4,1,512]{4,3,2,1,0:T(1,128)S(1)}) fusion(pred[]{:T(512)S(6)} %eq.58, f32[1,32,4,2,512]{4,3,2,1,0:T(2,128)S(1)} %exp.31, f32[1,32,4,2,512]{4,3,2,1,0:T(2,128)S(1)} %broadcast_select_fusion.1), kind=kLoop, calls=%fused_computation.11 | loop fusion | flops 393216 | bytes 2621441 | tf_op jit(solution)/shard_map/jit(_where)/select_n | solution.py:50
  31.3 0.1 copy.64
  31.5 1.6 %collective-permute-start = (f32[2,32,4,512]{3,2,1,0:T(4,128)S(1)}, f32[2,32,4,512]{3,2,1,0:T(4,128)S(1)}, u32[]{:S(2)}, u32[]{:S(2)}) collective-permute-start(f32[2,32,4,512]{3,2,1,0:T(4,128)S(1)} %bitcast.78), channel_id=1, source_target_pairs={{0,1},{1,0},{2,3},{3,2},{4,5},{5,4},{6,7},{7,6},{8,9},{9,8},{10,11... | collective-permute-start | bytes 1572872 | tf_op jit(solution)/shard_map/ppermute | solution.py:20
  33.0 12.7 %collective-permute-done = f32[2,32,4,512]{3,2,1,0:T(4,128)S(1)} collective-permute-done((f32[2,32,4,512]{3,2,1,0:T(4,128)S(1)}, f32[2,32,4,512]{3,2,1,0:T(4,128)S(1)}, u32[]{:S(2)}, u32[]{:S(2)}) %collective-permute-start) | collective-permute-done | bytes 524320 | tf_op jit(solution)/shard_map/ppermute | solution.py:20
  45.7 0.3 broadcast_select_fusion.3
  46.0 0.1 fusion.9
  46.2 0.1 copy.37
  46.3 0.1 copy.38
  46.4 1.7 %collective-permute-start.1 = (f32[2,32,2,512]{3,1,2,0:T(8,128)S(1)}, f32[2,32,2,512]{3,1,2,0:T(8,128)S(1)}, u32[]{:S(2)}, u32[]{:S(2)}) collective-permute-start(f32[2,32,2,512]{3,1,2,0:T(8,128)S(1)} %select_bitcast_fusion), channel_id=1, source_target_pairs={{0,2},{1,3},{2,0},{3,1},{4,6},{5,7},{6,4},{7,5},{8,10},{9,11},{10,... | collective-permute-start | bytes 786440 | tf_op jit(solution)/shard_map/ppermute | solution.py:20
  48.0 6.2 %collective-permute-done.1 = f32[2,32,2,512]{3,1,2,0:T(8,128)S(1)} collective-permute-done((f32[2,32,2,512]{3,1,2,0:T(8,128)S(1)}, f32[2,32,2,512]{3,1,2,0:T(8,128)S(1)}, u32[]{:S(2)}, u32[]{:S(2)}) %collective-permute-start.1) | collective-permute-done | bytes 262176 | tf_op jit(solution)/shard_map/ppermute | solution.py:20
  54.2 0.1 broadcast_select_fusion.5
  54.4 2.7 %collective-permute-start.2 = (f32[2,32,1,512]{3,1,0,2:T(8,128)S(1)}, f32[2,32,1,512]{3,1,0,2:T(8,128)S(1)}, u32[]{:S(2)}, u32[]{:S(2)}) collective-permute-start(f32[2,32,1,512]{3,1,0,2:T(8,128)S(1)} %select_bitcast_fusion.1), channel_id=1, source_target_pairs={{0,4},{1,5},{2,6},{3,7},{4,0},{5,1},{6,2},{7,3},{8,12},{9,13},{10,... | collective-permute-start | bytes 393224 | tf_op jit(solution)/shard_map/ppermute | solution.py:20
  57.1 5.1 %collective-permute-done.2 = f32[2,32,1,512]{3,1,0,2:T(8,128)S(1)} collective-permute-done((f32[2,32,1,512]{3,1,0,2:T(8,128)S(1)}, f32[2,32,1,512]{3,1,0,2:T(8,128)S(1)}, u32[]{:S(2)}, u32[]{:S(2)}) %collective-permute-start.2) | collective-permute-done | bytes 131104 | tf_op jit(solution)/shard_map/ppermute | solution.py:20
  62.3 0.1 broadcast_select_fusion.7
  62.3 0.7 %fusion.13 = (f32[32,512]{1,0:T(8,128)}, f32[32,512]{1,0:T(8,128)}) fusion(f32[2,32,1,512]{3,1,0,2:T(8,128)S(1)} %get-tuple-element.122, f32[2,32,1,512]{3,1,0,2:T(8,128)S(1)} %get-tuple-element.121), kind=kLoop, calls=%fused_computation.42 | loop fusion | flops 49152 | bytes 393216 | tf_op jit(solution)/shard_map/mul | solution.py:56
  (6 shorter events, 0.1 us)
Async XLA Ops:
  13.0 6.6 %copy-start = (f32[32,4,4096]{2,1,0:T(4,128)S(1)}, f32[32,4,4096]{2,1,0:T(4,128)}, u32[]{:S(2)}) copy-start(f32[32,4,4096]{2,1,0:T(4,128)} %param.5) | copy-start | bytes 6291460
  27.4 2.0 %copy-start.1 = (f32[32,4096]{1,0:T(8,128)S(1)}, f32[32,4096]{1,0:T(8,128)}, u32[]{:S(2)}) copy-start(f32[32,4096]{1,0:T(8,128)} %negate_exponential_fusion) | copy-start | bytes 1572868
  27.4 2.5 %copy-start.2 = (s32[32]{0:T(128)S(1)}, s32[32]{0:T(128)}, u32[]{:S(2)}) copy-start(s32[32]{0:T(128)} %param.7) | copy-start | bytes 388
  31.5 14.2 %collective-permute-start = (f32[2,32,4,512]{3,2,1,0:T(4,128)S(1)}, f32[2,32,4,512]{3,2,1,0:T(4,128)S(1)}, u32[]{:S(2)}, u32[]{:S(2)}) collective-permute-start(f32[2,32,4,512]{3,2,1,0:T(4,128)S(1)} %bitcast.78), channel_id=1, source_target_pairs={{0,1},{1,0},{2,3},{3,2},{4,5},{5,4},{6,7},{7,6},{8,9},{9,8},{10,11... | collective-permute-start | bytes 1572872 | tf_op jit(solution)/shard_map/ppermute | solution.py:20
  46.4 7.8 %collective-permute-start.1 = (f32[2,32,2,512]{3,1,2,0:T(8,128)S(1)}, f32[2,32,2,512]{3,1,2,0:T(8,128)S(1)}, u32[]{:S(2)}, u32[]{:S(2)}) collective-permute-start(f32[2,32,2,512]{3,1,2,0:T(8,128)S(1)} %select_bitcast_fusion), channel_id=1, source_target_pairs={{0,2},{1,3},{2,0},{3,1},{4,6},{5,7},{6,4},{7,5},{8,10},{9,11},{10,... | collective-permute-start | bytes 786440 | tf_op jit(solution)/shard_map/ppermute | solution.py:20
  54.4 7.8 %collective-permute-start.2 = (f32[2,32,1,512]{3,1,0,2:T(8,128)S(1)}, f32[2,32,1,512]{3,1,0,2:T(8,128)S(1)}, u32[]{:S(2)}, u32[]{:S(2)}) collective-permute-start(f32[2,32,1,512]{3,1,0,2:T(8,128)S(1)} %select_bitcast_fusion.1), channel_id=1, source_target_pairs={{0,4},{1,5},{2,6},{3,7},{4,0},{5,1},{6,2},{7,3},{8,12},{9,13},{10,... | collective-permute-start | bytes 393224 | tf_op jit(solution)/shard_map/ppermute | solution.py:20
where the time goes:
time: 63.3 us; the launch traced here: 63 us
  waiting for transfers between devices  24 us (38%)
  other arithmetic  22.4 us (35%)
  blocking collectives  7.22 us (11%)
  starting transfers between devices  5.89 us (9%)
  local copies, waits for them, and re-layouts  2.74 us (4%)
  between operations  0.8 us (1%)
    ppermute x3, waiting for transfers between devices, swapped(): lax.ppermute(value, axis, [(i, i ^ 1 << bit) for i in range(lax.axis_size...  24 us
    another operation x1, other arithmetic, shards(): depth = incoming[None] + (jnp.cumsum(tau_light, axis=0) - tau_light)  7.72 us
    all_gather x1, blocking collectives, entering(): pieces = lax.all_gather(value, axis)  7.22 us
    another operation x1, other arithmetic, shards(): running = jnp.cumsum(tau_view, axis=1)  6.63 us
    ppermute x3, starting transfers between devices, swapped(): lax.ppermute(value, axis, [(i, i ^ 1 << bit) for i in range(lax.axis_size...  5.89 us
    reduce_sum x1, other arithmetic, shards(): slab_depth = jnp.sum(tau_light, axis=0)  4.02 us
    reduce_sum x1, local copies, waits for them, and re-layouts, shards(): backward = jnp.sum(lit * jnp.exp(-(total[:, None, :] - running)), axis=1)  1.54 us
  transfers between devices with their start and end apart: 3, of which 3 were waited for; matrix products, arithmetic and copies ran while one was open for 0% of the time, Pallas kernels for 0%

commit v1 on v0

v1 whole, which is shorter than its diff:
```python
import functools

import jax
import jax.numpy as jnp
from jax import lax
from jax.experimental import pallas as pl
from jax.experimental.pallas import tpu as pltpu
from jax.sharding import PartitionSpec as P

LANES = 128
SUB = 8
CHUNKS = 4
MESH = pl.DeviceIdType.MESH


def transposed(regs, width, block):
    regs, bit = list(regs), 1
    while bit < len(regs):
        low = (block & bit) == 0
        for i in range(len(regs)):
            if i & bit == 0:
                a, b = regs[i], regs[i | bit]
                regs[i] = jnp.where(low, a, pltpu.roll(b, bit * width, 0))
                regs[i | bit] = jnp.where(low, pltpu.roll(a, SUB - bit * width, 0), b)
        bit *= 2
    return regs


def kernel(
    rows, cells, columns, lights, views,
    facing, dens_hbm, emis_hbm, radiance, coverage,
    dens, emis, slab, slabs, incoming, msg, xbuf, comb, zbuf,
    load_sem, light_send, light_recv, x_send, x_recv, z_send, z_recv,
):
    light, view = lax.axis_index("light"), lax.axis_index("view")
    x, z = lax.rem(view, 2), lax.div(view, 2)
    deep = views // 2
    tiles = columns // (SUB * LANES)
    width = columns // (views * LANES)
    n = SUB // width
    groups = rows // n
    light_scale = 1.0 / (rows * lights)
    view_scale = 1.0 / (cells * views)
    power = (rows * lights) // (cells * views)
    whole_power = power * cells * views == rows * lights
    pitch = columns // LANES * cells
    part = rows * pitch // CHUNKS
    per_chunk = groups // CHUNKS
    order = list(range(1, deep)) + [0]

    loads = [
        [
            pltpu.make_async_copy(
                source.at[pl.ds(k * part, part)], target.at[pl.ds(k * part, part)], load_sem.at[t, k]
            )
            for k in range(CHUNKS)
        ]
        for t, (source, target) in enumerate(((dens_hbm, dens), (emis_hbm, emis)))
    ]
    for copy in loads[0] + loads[1]:
        copy.start()

    barrier = pltpu.get_barrier_semaphore()
    for d in range(1, lights):
        pl.semaphore_signal(
            barrier, inc=1, device_id={"light": lax.rem(light + d, lights)}, device_id_type=MESH
        )
    pl.semaphore_signal(barrier, inc=1, device_id={"view": view + 1 - 2 * x}, device_id_type=MESH)
    for q in range(1, deep):
        pl.semaphore_signal(
            barrier, inc=1, device_id={"view": lax.rem(z + q, deep) * 2 + x}, device_id_type=MESH
        )

    block = lax.broadcasted_iota(jnp.int32, (SUB, LANES), 0) // width

    def tile(ref, row, m, v):
        return ref[pl.ds(row * pitch + m * SUB * cells + v, SUB, stride=cells), :]

    def turned(g):
        mask = jnp.full((SUB, LANES), facing[g * n], jnp.int32)
        for i in range(1, n):
            mask = jnp.where(block == i, facing[g * n + i], mask)
        return mask

    def first(g, sums):
        sums = list(sums)
        for m in range(tiles):
            totals = []
            for i in range(n):
                total = None
                for v in range(cells):
                    d = tile(dens, g * n + i, m, v)
                    sums[m * cells + v] = sums[m * cells + v] + d
                    total = d if total is None else total + d
                totals.append(jnp.exp(total * -view_scale))
            for o, packed in enumerate(transposed(totals, width, block)):
                msg[0, m * n + o, g] = packed
        return tuple(sums)

    sums = tuple(jnp.zeros((SUB, LANES), jnp.float32) for _ in range(tiles * cells))
    for k in range(CHUNKS):
        loads[0][k].wait()
        sums = lax.fori_loop(k * per_chunk, (k + 1) * per_chunk, first, sums)
    for j in range(tiles * cells):
        slab[j] = sums[j]

    pl.semaphore_wait(barrier, lights - 1 + 1 + deep - 1)

    def to_light(d):
        return pltpu.make_async_remote_copy(
            src_ref=slab,
            dst_ref=slabs.at[d - 1],
            send_sem=light_send.at[d - 1],
            recv_sem=light_recv.at[d - 1],
            device_id={"light": lax.rem(light + d, lights)},
            device_id_type=MESH,
        )

    def to_x(t, q):
        owner = lax.rem(z + q, deep) * 2
        return pltpu.make_async_remote_copy(
            src_ref=msg.at[t, owner + 1 - x],
            dst_ref=xbuf.at[t, q],
            send_sem=x_send.at[t, q],
            recv_sem=x_recv.at[t, q],
            device_id={"view": view + 1 - 2 * x},
            device_id_type=MESH,
        )

    def to_z(t, q):
        return pltpu.make_async_remote_copy(
            src_ref=comb.at[t, q - 1],
            dst_ref=zbuf.at[t, q],
            send_sem=z_send.at[t, q],
            recv_sem=z_recv.at[t, q],
            device_id={"view": lax.rem(z + q, deep) * 2 + x},
            device_id_type=MESH,
        )

    for d in reversed(range(1, lights)):
        @pl.when(light + d < lights)
        def _():
            to_light(d).start()
    for q in order:
        to_x(0, q).start()

    def join_trans(q):
        owner = lax.rem(z + q, deep) * 2 + x
        to_x(0, q).wait_recv()

        def step(g, carry):
            value = msg[0, owner, g] * xbuf[0, q, g]
            if q:
                comb[0, q - 1, g] = value
            else:
                zbuf[0, 0, g] = value
            return carry

        lax.fori_loop(0, groups, step, 0)
        if q:
            to_z(0, q).start()

    def join_color(q):
        owner = lax.rem(z + q, deep) * 2 + x
        to_x(1, q).wait_recv()

        def step(g, carry):
            mine, other = msg[1, owner, g], xbuf[1, q, g]
            value = jnp.where(
                turned(g) == x, mine + msg[0, owner, g] * other, other + xbuf[0, q, g] * mine
            )
            if q:
                comb[1, q - 1, g] = value
            else:
                zbuf[1, 0, g] = value
            return carry

        lax.fori_loop(0, groups, step, 0)
        if q:
            to_z(1, q).start()

    early = deep // 2
    for q in order[:early]:
        join_trans(q)

    incoming[...] = jnp.zeros_like(incoming)
    for d in range(1, lights):
        @pl.when(light >= d)
        def _():
            to_light(d).wait_recv()
            incoming[...] += slabs[d - 1]

    def second(g, lights_in):
        lights_in = list(lights_in)
        swap = [facing[g * n + i] == 1 for i in range(n)]
        for m in range(tiles):
            colors = []
            for i in range(n):
                lit, through = [], []
                for v in range(cells):
                    d = tile(dens, g * n + i, m, v)
                    thin = jnp.exp(d * -light_scale)
                    passed = lax.integer_pow(thin, power) if whole_power else jnp.exp(d * -view_scale)
                    reach = lights_in[m * cells + v]
                    lit.append(tile(emis, g * n + i, m, v) * (0.2 + reach) * (1.0 - passed))
                    through.append(passed)
                    lights_in[m * cells + v] = reach * thin
                forward, backward = lit[-1], lit[0]
                for v in range(cells - 2, -1, -1):
                    forward = lit[v] + through[v] * forward
                for v in range(1, cells):
                    backward = lit[v] + through[v] * backward
                colors.append(jnp.where(swap[i], backward, forward))
            for o, packed in enumerate(transposed(colors, width, block)):
                msg[1, m * n + o, g] = packed
        return tuple(lights_in)

    lights_in = tuple(jnp.exp(incoming[j] * -light_scale) for j in range(tiles * cells))
    for k in range(CHUNKS):
        loads[1][k].wait()
        lights_in = lax.fori_loop(k * per_chunk, (k + 1) * per_chunk, second, lights_in)
    for q in order:
        to_x(1, q).start()

    for q in order[early:]:
        join_trans(q)
    for q in order:
        join_color(q)
    for q in range(1, deep):
        for t in range(2):
            to_z(t, q).wait_recv()

    def last(g, carry):
        color = [None] * deep
        trans = [None] * deep
        for at in range(deep):
            slot = lax.rem(z + deep - at, deep)
            trans[at], color[at] = zbuf[0, slot, g], zbuf[1, slot, g]
        forward, backward, total = color[-1], color[0], trans[0]
        for at in range(deep - 2, -1, -1):
            forward = color[at] + trans[at] * forward
        for at in range(1, deep):
            backward = color[at] + trans[at] * backward
            total = total * trans[at]
        radiance[g] = jnp.where(turned(g) == 1, backward, forward)
        coverage[g] = total
        return carry

    lax.fori_loop(0, groups, last, 0)

    for d in range(1, lights):
        @pl.when(light + d < lights)
        def _():
            to_light(d).wait_send()
    for t in range(2):
        for q in range(deep):
            to_x(t, q).wait_send()
            if q:
                to_z(t, q).wait_send()


def shards(density, emission, facing):
    rows, cells, columns = density.shape
    lights, views = lax.axis_size("light"), lax.axis_size("view")
    deep = views // 2
    width = columns // (views * LANES)
    groups = rows * width // SUB
    tiles = columns // (SUB * LANES)

    def linear(a):
        a = a.reshape(rows, cells, columns // LANES, LANES)
        return a.transpose(0, 2, 1, 3).reshape(-1, LANES)

    f32 = jnp.float32
    piece = (groups, SUB, LANES)
    lines = rows * cells * columns // LANES
    radiance, coverage = pl.pallas_call(
        functools.partial(kernel, rows, cells, columns, lights, views),
        out_shape=[jax.ShapeDtypeStruct(piece, f32)] * 2,
        in_specs=[
            pl.BlockSpec(memory_space=pltpu.SMEM),
            pl.BlockSpec(memory_space=pltpu.HBM),
            pl.BlockSpec(memory_space=pltpu.HBM),
        ],
        out_specs=[pl.BlockSpec(memory_space=pltpu.VMEM)] * 2,
        scratch_shapes=[
            pltpu.VMEM((lines, LANES), f32),
            pltpu.VMEM((lines, LANES), f32),
            pltpu.VMEM((tiles * cells, SUB, LANES), f32),
            pltpu.VMEM((lights - 1, tiles * cells, SUB, LANES), f32),
            pltpu.VMEM((tiles * cells, SUB, LANES), f32),
            pltpu.VMEM((2, views) + piece, f32),
            pltpu.VMEM((2, deep) + piece, f32),
            pltpu.VMEM((2, deep - 1) + piece, f32),
            pltpu.VMEM((2, deep) + piece, f32),
            pltpu.SemaphoreType.DMA((2, CHUNKS)),
            pltpu.SemaphoreType.DMA((lights - 1,)),
            pltpu.SemaphoreType.DMA((lights - 1,)),
            pltpu.SemaphoreType.DMA((2, deep)),
            pltpu.SemaphoreType.DMA((2, deep)),
            pltpu.SemaphoreType.DMA((2, deep)),
            pltpu.SemaphoreType.DMA((2, deep)),
        ],
        compiler_params=pltpu.CompilerParams(
            collective_id=0, has_side_effects=True, vmem_limit_bytes=48 * 2**20
        ),
    )(facing, linear(density), linear(emission))
    return radiance.reshape(rows, width * LANES), coverage.reshape(rows, width * LANES)


def solution(mesh):
    return jax.shard_map(
        shards,
        mesh=mesh,
        in_specs=(P("light", "view", None), P("light", "view", None), P("light")),
        out_specs=(P("light", "view"), P("light", "view")),
        check_vma=False,
    )
```

time: 63.3 us -> 29.1 us (0.46)
  waiting for transfers between devices: 24 us -> 0 us
  Pallas kernels: 0 us -> 23.1 us
  other arithmetic: 22.4 us -> 0 us
  blocking collectives: 7.22 us -> 0 us
  starting transfers between devices: 5.89 us -> 0 us
  local copies, waits for them, and re-layouts: 2.74 us -> 5.11 us
    ppermute x3 -> x0, waiting for transfers between devices: 24 us -> none  [swapped(): lax.ppermute(value, axis, [(i, i ^ 1 << bit) for i in range(lax.axis_size...]
    pallas_call x0 -> x1, Pallas kernels: none -> 23.1 us  [shards(): pl.pallas_call(functools.partial(kernel, rows, cells, columns, lights, vi...]
    another operation x2 -> x0, other arithmetic: 14.3 us -> none  [the longest x1 7.72 us: shards(): depth = incoming[None] + (jnp.cumsum(tau_light, axis=0) - tau_light)]
    all_gather x1 -> x0, blocking collectives: 7.22 us -> none  [entering(): pieces = lax.all_gather(value, axis)]
    ppermute x3 -> x0, starting transfers between devices: 5.89 us -> none  [swapped(): lax.ppermute(value, axis, [(i, i ^ 1 << bit) for i in range(lax.axis_size...]
    reduce_sum x1 -> x0, other arithmetic: 4.02 us -> none  [shards(): slab_depth = jnp.sum(tau_light, axis=0)]
    unnamed x7 -> x6, local copies, waits for them, and re-layouts: 0.15 us -> 3.83 us
    select_n x10 -> x0, other arithmetic: 2.24 us -> none  [the longest x3 1.19 us: shards(): send_part = jnp.where(my_bit == 1, paired[:, :, :, 0], paired[:, :, :, 1])]
  transfers between devices with their start and end apart: 3 -> 0, of which waited for: 3 -> 0; matrix products, arithmetic and copies ran while one was open for 0% -> 0% of each run, Pallas kernels for 0% -> 0%
where the time goes in v1:
time: 29.1 us; the launch traced here: 28.9 us
  Pallas kernels  23.1 us (79%)
  local copies, waits for them, and re-layouts  5.11 us (18%)
  between operations  0.65 us (2%)
    pallas_call x1, Pallas kernels, shards(): pl.pallas_call(functools.partial(kernel, rows, cells, columns, lights, vi...  23.1 us
    unnamed x6, local copies, waits for them, and re-layouts  3.83 us
    reshape x1, local copies, waits for them, and re-layouts, shards(): radiance.reshape(rows, width * LANES)  0.64 us
    reshape x1, local copies, waits for them, and re-layouts, shards(): coverage.reshape(rows, width * LANES)  0.64 us

profile of v1, /device:TPU:0, one launch (start us, length us, event | category | flops | bytes accessed | tf_op | source)
XLA Modules:
  0.0 28.9 jit_solution(7361976429400453246)
XLA Ops:
  0.6 0.0 copy-start
  0.6 1.6 %copy-done = f32[32,4,4096]{2,1,0:T(4,128)S(1)} copy-done((f32[32,4,4096]{2,1,0:T(4,128)S(1)}, f32[32,4,4096]{2,1,0:T(4,128)}, u32[]{:S(2)}) %copy-start) | copy-done | bytes 2097176
  2.2 0.0 copy-start.1
  2.2 1.6 %copy-done.1 = f32[32,4,4096]{2,1,0:T(4,128)S(1)} copy-done((f32[32,4,4096]{2,1,0:T(4,128)S(1)}, f32[32,4,4096]{2,1,0:T(4,128)}, u32[]{:S(2)}) %copy-start.1) | copy-done | bytes 2097176
  3.8 0.0 copy-start.2
  3.8 0.7 %copy-done.2 = s32[32]{0:T(128)S(1)} copy-done((s32[32]{0:T(128)S(1)}, s32[32]{0:T(128)}, u32[]{:S(2)}) %copy-start.2) | copy-done | bytes 152
  4.5 23.1 %shard_map.50 = (f32[16,8,128]{2,1,0:T(8,128)S(1)}, f32[16,8,128]{2,1,0:T(8,128)S(1)}) custom-call(s32[32]{0:T(128)S(1)} %copy-done.2, f32[4096,128]{1,0:T(8,128)S(1)} %bitcast.10, f32[4096,128]{1,0:T(8,128)S(1)} %bitcast.11), custom_call_target="tpu_custom_call" | custom-call | tf_op jit(solution)/shard_map/pallas_call | solution.py:277
  27.6 0.6 %reshape.26 = f32[32,512]{1,0:T(8,128)} reshape(f32[16,8,128]{2,1,0:T(8,128)S(1)} %get-tuple-element.4) | data formatting | bytes 131072 | tf_op jit(solution)/shard_map/reshape | solution.py:308
  28.2 0.6 %reshape.27 = f32[32,512]{1,0:T(8,128)} reshape(f32[16,8,128]{2,1,0:T(8,128)S(1)} %get-tuple-element.5) | data formatting | bytes 131072 | tf_op jit(solution)/shard_map/reshape | solution.py:308
Async XLA Ops:
  0.6 1.6 %copy-start = (f32[32,4,4096]{2,1,0:T(4,128)S(1)}, f32[32,4,4096]{2,1,0:T(4,128)}, u32[]{:S(2)}) copy-start(f32[32,4,4096]{2,1,0:T(4,128)} %param.3) | copy-start | bytes 6291460
  2.2 1.6 %copy-start.1 = (f32[32,4,4096]{2,1,0:T(4,128)S(1)}, f32[32,4,4096]{2,1,0:T(4,128)}, u32[]{:S(2)}) copy-start(f32[32,4,4096]{2,1,0:T(4,128)} %param.4) | copy-start | bytes 6291460
  3.8 0.7 %copy-start.2 = (s32[32]{0:T(128)S(1)}, s32[32]{0:T(128)}, u32[]{:S(2)}) copy-start(s32[32]{0:T(128)} %facing.1) | copy-start | bytes 388

commit v2 on v1

v2 whole, which is shorter than its diff:
```python
import functools

import jax
import jax.numpy as jnp
from jax import lax
from jax.experimental import pallas as pl
from jax.experimental.pallas import tpu as pltpu
from jax.sharding import PartitionSpec as P

LANES = 128
SUB = 8
MESH = pl.DeviceIdType.MESH


def transposed(regs, width, block):
    regs, bit = list(regs), 1
    while bit < len(regs):
        low = (block & bit) == 0
        for i in range(len(regs)):
            if i & bit == 0:
                a, b = regs[i], regs[i | bit]
                regs[i] = jnp.where(low, a, pltpu.roll(b, bit * width, 0))
                regs[i | bit] = jnp.where(low, pltpu.roll(a, SUB - bit * width, 0), b)
        bit *= 2
    return regs


def kernel(
    rows, cells, columns, lights, views,
    facing, dens_hbm, emis_hbm, radiance, coverage,
    dens, emis, slab, slabs, incoming, msg, xbuf, comb, zbuf,
    load_sem, light_send, light_recv, x_send, x_recv, z_send, z_recv,
):
    light, view = lax.axis_index("light"), lax.axis_index("view")
    x, z = lax.rem(view, 2), lax.div(view, 2)
    deep = views // 2
    tiles = columns // (SUB * LANES)
    width = columns // (views * LANES)
    n = SUB // width
    groups = rows // n
    light_scale = 1.0 / (rows * lights)
    view_scale = 1.0 / (cells * views)
    power = (rows * lights) // (cells * views)
    whole_power = power * cells * views == rows * lights
    lines = SUB * cells
    per_tile = deep // tiles
    order = list(range(1, deep)) + [0]
    first_tile = lax.div(z, per_tile)
    visits = [lax.rem(first_tile + k, tiles) for k in list(range(1, tiles)) + [0]]

    loads = [
        [
            pltpu.make_async_copy(
                source.at[:, pl.ds(pl.multiple_of(m * lines, SUB), lines), :], target.at[k], load_sem.at[t, k]
            )
            for k, m in enumerate(visits)
        ]
        for t, (source, target) in enumerate(((dens_hbm, dens), (emis_hbm, emis)))
    ]
    for copy in loads[0] + loads[1]:
        copy.start()

    barrier = pltpu.get_barrier_semaphore()
    for d in range(1, lights):
        pl.semaphore_signal(
            barrier, inc=1, device_id={"light": lax.rem(light + d, lights)}, device_id_type=MESH
        )
    pl.semaphore_signal(barrier, inc=1, device_id={"view": view + 1 - 2 * x}, device_id_type=MESH)
    for q in range(1, deep):
        pl.semaphore_signal(
            barrier, inc=1, device_id={"view": lax.rem(z + q, deep) * 2 + x}, device_id_type=MESH
        )

    block = lax.broadcasted_iota(jnp.int32, (SUB, LANES), 0) // width

    def tile(ref, k, row, v):
        return ref[k, row, pl.ds(v, SUB, stride=cells), :]

    def turned(g):
        mask = jnp.full((SUB, LANES), facing[g * n], jnp.int32)
        for i in range(1, n):
            mask = jnp.where(block == i, facing[g * n + i], mask)
        return mask

    def first(k, m, g, sums):
        sums, totals = list(sums), []
        for i in range(n):
            total = None
            for v in range(cells):
                d = tile(dens, k, g * n + i, v)
                sums[v] = sums[v] + d
                total = d if total is None else total + d
            totals.append(jnp.exp(total * -view_scale))
        for o, packed in enumerate(transposed(totals, width, block)):
            msg[0, m * n + o, g] = packed
        return tuple(sums)

    def to_light(d, k):
        return pltpu.make_async_remote_copy(
            src_ref=slab.at[k],
            dst_ref=slabs.at[d - 1, k],
            send_sem=light_send.at[d - 1, k],
            recv_sem=light_recv.at[d - 1, k],
            device_id={"light": lax.rem(light + d, lights)},
            device_id_type=MESH,
        )

    def to_x(t, q):
        owner = lax.rem(z + q, deep) * 2
        return pltpu.make_async_remote_copy(
            src_ref=msg.at[t, owner + 1 - x],
            dst_ref=xbuf.at[t, q],
            send_sem=x_send.at[t, q],
            recv_sem=x_recv.at[t, q],
            device_id={"view": view + 1 - 2 * x},
            device_id_type=MESH,
        )

    def to_z(t, q):
        return pltpu.make_async_remote_copy(
            src_ref=comb.at[t, q - 1],
            dst_ref=zbuf.at[t, q],
            send_sem=z_send.at[t, q],
            recv_sem=z_recv.at[t, q],
            device_id={"view": lax.rem(z + q, deep) * 2 + x},
            device_id_type=MESH,
        )

    def send_x(t, m):
        for i in list(range(1, per_tile)) + [0]:
            to_x(t, lax.rem(m * per_tile + i - z + deep, deep)).start()

    zeros = tuple(jnp.zeros((SUB, LANES), jnp.float32) for _ in range(cells))
    for k, m in enumerate(visits):
        loads[0][k].wait()
        sums = lax.fori_loop(0, groups, functools.partial(first, k, m), zeros, unroll=2)
        for v in range(cells):
            slab[k, v] = sums[v]
        if k == 0:
            pl.semaphore_wait(barrier, lights - 1 + 1 + deep - 1)
        for d in reversed(range(1, lights)):
            @pl.when(light + d < lights)
            def _():
                to_light(d, k).start()
        send_x(0, m)

    def join_trans(q):
        owner = lax.rem(z + q, deep) * 2 + x
        to_x(0, q).wait_recv()

        def step(g, carry):
            value = msg[0, owner, g] * xbuf[0, q, g]
            if q:
                comb[0, q - 1, g] = value
            else:
                zbuf[0, 0, g] = value
            return carry

        lax.fori_loop(0, groups, step, 0, unroll=min(4, groups))
        if q:
            to_z(0, q).start()

    def join_color(q):
        owner = lax.rem(z + q, deep) * 2 + x
        to_x(1, q).wait_recv()

        def step(g, carry):
            mine, other = msg[1, owner, g], xbuf[1, q, g]
            value = jnp.where(
                turned(g) == x, mine + msg[0, owner, g] * other, other + xbuf[0, q, g] * mine
            )
            if q:
                comb[1, q - 1, g] = value
            else:
                zbuf[1, 0, g] = value
            return carry

        lax.fori_loop(0, groups, step, 0, unroll=min(4, groups))
        if q:
            to_z(1, q).start()

    def second(k, m, g, lights_in):
        lights_in, colors = list(lights_in), []
        for i in range(n):
            lit, through = [], []
            for v in range(cells):
                d = tile(dens, k, g * n + i, v)
                thin = jnp.exp(d * -light_scale)
                passed = lax.integer_pow(thin, power) if whole_power else jnp.exp(d * -view_scale)
                lit.append(tile(emis, k, g * n + i, v) * (0.2 + lights_in[v]) * (1.0 - passed))
                through.append(passed)
                lights_in[v] = lights_in[v] * thin
            forward, backward = lit[-1], lit[0]
            for v in range(cells - 2, -1, -1):
                forward = lit[v] + through[v] * forward
            for v in range(1, cells):
                backward = lit[v] + through[v] * backward
            colors.append(jnp.where(facing[g * n + i] == 1, backward, forward))
        for o, packed in enumerate(transposed(colors, width, block)):
            msg[1, m * n + o, g] = packed
        return tuple(lights_in)

    incoming[...] = jnp.zeros_like(incoming)
    for k, m in enumerate(visits):
        for d in range(1, lights):
            @pl.when(light >= d)
            def _():
                to_light(d, k).wait_recv()
                incoming[k] += slabs[d - 1, k]
        loads[1][k].wait()
        lights_in = tuple(jnp.exp(incoming[k, v] * -light_scale) for v in range(cells))
        lax.fori_loop(0, groups, functools.partial(second, k, m), lights_in, unroll=2)
        send_x(1, m)
        for q in order[k * per_tile : (k + 1) * per_tile]:
            join_trans(q)
    for q in order:
        join_color(q)
    for q in range(1, deep):
        for t in range(2):
            to_z(t, q).wait_recv()

    def last(g, carry):
        color = [None] * deep
        trans = [None] * deep
        for at in range(deep):
            slot = lax.rem(z + deep - at, deep)
            trans[at], color[at] = zbuf[0, slot, g], zbuf[1, slot, g]
        forward, backward, total = color[-1], color[0], trans[0]
        for at in range(deep - 2, -1, -1):
            forward = color[at] + trans[at] * forward
        for at in range(1, deep):
            backward = color[at] + trans[at] * backward
            total = total * trans[at]
        radiance[g] = jnp.where(turned(g) == 1, backward, forward)
        coverage[g] = total
        return carry

    lax.fori_loop(0, groups, last, 0, unroll=2)

    for d in range(1, lights):
        @pl.when(light + d < lights)
        def _():
            for k in range(tiles):
                to_light(d, k).wait_send()
    for t in range(2):
        for q in range(deep):
            to_x(t, q).wait_send()
            if q:
                to_z(t, q).wait_send()


def shards(density, emission, facing):
    rows, cells, columns = density.shape
    lights, views = lax.axis_size("light"), lax.axis_size("view")
    deep = views // 2
    width = columns // (views * LANES)
    groups = rows * width // SUB
    tiles = columns // (SUB * LANES)

    def linear(a):
        a = a.reshape(rows, cells, columns // LANES, LANES)
        return a.transpose(0, 2, 1, 3).reshape(rows, -1, LANES)

    f32 = jnp.float32
    piece = (groups, SUB, LANES)
    field = (tiles, rows, SUB * cells, LANES)
    radiance, coverage = pl.pallas_call(
        functools.partial(kernel, rows, cells, columns, lights, views),
        out_shape=[jax.ShapeDtypeStruct(piece, f32)] * 2,
        in_specs=[
            pl.BlockSpec(memory_space=pltpu.SMEM),
            pl.BlockSpec(memory_space=pltpu.HBM),
            pl.BlockSpec(memory_space=pltpu.HBM),
        ],
        out_specs=[pl.BlockSpec(memory_space=pltpu.VMEM)] * 2,
        scratch_shapes=[
            pltpu.VMEM(field, f32),
            pltpu.VMEM(field, f32),
            pltpu.VMEM((tiles, cells, SUB, LANES), f32),
            pltpu.VMEM((lights - 1, tiles, cells, SUB, LANES), f32),
            pltpu.VMEM((tiles, cells, SUB, LANES), f32),
            pltpu.VMEM((2, views) + piece, f32),
            pltpu.VMEM((2, deep) + piece, f32),
            pltpu.VMEM((2, deep - 1) + piece, f32),
            pltpu.VMEM((2, deep) + piece, f32),
            pltpu.SemaphoreType.DMA((2, tiles)),
            pltpu.SemaphoreType.DMA((lights - 1, tiles)),
            pltpu.SemaphoreType.DMA((lights - 1, tiles)),
            pltpu.SemaphoreType.DMA((2, deep)),
            pltpu.SemaphoreType.DMA((2, deep)),
            pltpu.SemaphoreType.DMA((2, deep)),
            pltpu.SemaphoreType.DMA((2, deep)),
        ],
        compiler_params=pltpu.CompilerParams(
            collective_id=0, has_side_effects=True, vmem_limit_bytes=62 * 2**20
        ),
    )(facing, linear(density), linear(emission))
    return radiance.reshape(rows, width * LANES), coverage.reshape(rows, width * LANES)


def solution(mesh):
    return jax.shard_map(
        shards,
        mesh=mesh,
        in_specs=(P("light", "view", None), P("light", "view", None), P("light")),
        out_specs=(P("light", "view"), P("light", "view")),
        check_vma=False,
    )
```

time: 29.1 us -> 27.5 us (0.945)
  local copies, waits for them, and re-layouts: 5.11 us -> 2.96 us
  Pallas kernels: 23.1 us -> 23.6 us
    unnamed x6 -> x0, local copies, waits for them, and re-layouts: 3.83 us -> none
    reshape x1, local copies, waits for them, and re-layouts: 0.64 us -> 1.48 us  [shards(): radiance.reshape(rows, width * LANES)]
    reshape x1, local copies, waits for them, and re-layouts: 0.64 us -> 1.48 us  [shards(): coverage.reshape(rows, width * LANES)]
    pallas_call x1, Pallas kernels: 23.1 us -> 23.6 us  [shards(): pl.pallas_call(functools.partial(kernel, rows, cells, columns, lights, vi...]
where the time goes in v2:
time: 27.5 us; the launch traced here: 27.2 us
  Pallas kernels  23.6 us (86%)
  local copies, waits for them, and re-layouts  2.96 us (11%)
  between operations  0.64 us (2%)
    pallas_call x1, Pallas kernels, shards(): pl.pallas_call(functools.partial(kernel, rows, cells, columns, lights, vi...  23.6 us
    reshape x1, local copies, waits for them, and re-layouts, shards(): radiance.reshape(rows, width * LANES)  1.48 us
    reshape x1, local copies, waits for them, and re-layouts, shards(): coverage.reshape(rows, width * LANES)  1.48 us

profile of v2, /device:TPU:0, one launch (start us, length us, event | category | flops | bytes accessed | tf_op | source)
XLA Modules:
  0.0 27.2 jit_solution(2671126822032209970)
XLA Ops:
  0.6 23.6 %shard_map.50 = (f32[16,8,128]{2,1,0:T(8,128)}, f32[16,8,128]{2,1,0:T(8,128)}) custom-call(s32[32]{0:T(128)} %facing.1, f32[32,128,128]{2,1,0:T(8,128)} %bitcast.10, f32[32,128,128]{2,1,0:T(8,128)} %bitcast.11), custom_call_target="tpu_custom_call" | custom-call | tf_op jit(solution)/shard_map/pallas_call | solution.py:267
  24.3 1.5 %reshape.26 = f32[32,512]{1,0:T(8,128)} reshape(f32[16,8,128]{2,1,0:T(8,128)} %get-tuple-element.4) | data formatting | bytes 131072 | tf_op jit(solution)/shard_map/reshape | solution.py:298
  25.8 1.5 %reshape.27 = f32[32,512]{1,0:T(8,128)} reshape(f32[16,8,128]{2,1,0:T(8,128)} %get-tuple-element.5) | data formatting | bytes 131072 | tf_op jit(solution)/shard_map/reshape | solution.py:298

commit v3 on v2

--- a/solution.py
+++ b/solution.py
@@ -292,7 +292,7 @@
             pltpu.SemaphoreType.DMA((2, deep)),
         ],
         compiler_params=pltpu.CompilerParams(
-            collective_id=0, has_side_effects=True, vmem_limit_bytes=62 * 2**20
+            collective_id=0, has_side_effects=True, vmem_limit_bytes=52 * 2**20
         ),
     )(facing, linear(density), linear(emission))
     return radiance.reshape(rows, width * LANES), coverage.reshape(rows, width * LANES)

time: 27.5 us -> 25.6 us (0.931)
  local copies, waits for them, and re-layouts: 2.96 us -> 1.93 us
  Pallas kernels: 23.6 us -> 22.9 us
    reshape x1, local copies, waits for them, and re-layouts: 1.48 us -> 0.64 us  [shards(): radiance.reshape(rows, width * LANES)]
    reshape x1, local copies, waits for them, and re-layouts: 1.48 us -> 0.64 us  [shards(): coverage.reshape(rows, width * LANES)]
    pallas_call x1, Pallas kernels: 23.6 us -> 22.9 us  [shards(): pl.pallas_call(functools.partial(kernel, rows, cells, columns, lights, vi...]
    unnamed x0 -> x2, local copies, waits for them, and re-layouts: none -> 0.65 us
where the time goes in v3:
time: 25.6 us; the launch traced here: 25.4 us
  Pallas kernels  22.9 us (89%)
  local copies, waits for them, and re-layouts  1.93 us (8%)
  between operations  0.65 us (3%)
    pallas_call x1, Pallas kernels, shards(): pl.pallas_call(functools.partial(kernel, rows, cells, columns, lights, vi...  22.9 us
    unnamed x2, local copies, waits for them, and re-layouts  0.65 us
    reshape x1, local copies, waits for them, and re-layouts, shards(): radiance.reshape(rows, width * LANES)  0.64 us
    reshape x1, local copies, waits for them, and re-layouts, shards(): coverage.reshape(rows, width * LANES)  0.64 us

profile of v3, /device:TPU:0, one launch (start us, length us, event | category | flops | bytes accessed | tf_op | source)
XLA Modules:
  0.0 25.4 jit_solution(13869840826367348709)
XLA Ops:
  0.6 0.0 copy-start
  0.6 0.6 %copy-done = s32[32]{0:T(128)S(1)} copy-done((s32[32]{0:T(128)S(1)}, s32[32]{0:T(128)}, u32[]{:S(2)}) %copy-start) | copy-done | bytes 152
  1.3 22.9 %shard_map.50 = (f32[16,8,128]{2,1,0:T(8,128)S(1)}, f32[16,8,128]{2,1,0:T(8,128)S(1)}) custom-call(s32[32]{0:T(128)S(1)} %copy-done, f32[32,128,128]{2,1,0:T(8,128)} %bitcast.10, f32[32,128,128]{2,1,0:T(8,128)} %bitcast.11), custom_call_target="tpu_custom_call" | custom-call | tf_op jit(solution)/shard_map/pallas_call | solution.py:267
  24.1 0.6 %reshape.26 = f32[32,512]{1,0:T(8,128)} reshape(f32[16,8,128]{2,1,0:T(8,128)S(1)} %get-tuple-element.4) | data formatting | bytes 131072 | tf_op jit(solution)/shard_map/reshape | solution.py:298
  24.8 0.6 %reshape.27 = f32[32,512]{1,0:T(8,128)} reshape(f32[16,8,128]{2,1,0:T(8,128)S(1)} %get-tuple-element.5) | data formatting | bytes 131072 | tf_op jit(solution)/shard_map/reshape | solution.py:298
Async XLA Ops:
  0.6 0.7 %copy-start = (s32[32]{0:T(128)S(1)}, s32[32]{0:T(128)}, u32[]{:S(2)}) copy-start(s32[32]{0:T(128)} %facing.1) | copy-start | bytes 388
